TPU v7x, 32 devices: a whole 2x2x4 slice. The times are simulated.
32 devices in a mesh: req: 8 (over y, x, core), blk: 4 (over z).
Axes of the slice: x: 2, y: 2, z: 4, core: 2. Of those that a mesh axis runs over, the one named last changes fastest.
Arguments:
- x_img: bfloat16 [8, 1024, 1536], P('req', 'blk'), may hold values from -0.3 to 0.3
- x_txt: bfloat16 [8, 154, 1536], P('req'), may hold values from -6 to 6
- modulation: float32 [8, 7, 1536], P('req'), may hold values from -8 to 8
- w_img: bfloat16 [1536, 2304], P(None, 'req'), may hold values from -0.375 to 0.375
- w_txt: bfloat16 [1536, 1536], P(None, 'req'), may hold values from -0.15625 to 0.15625
- w_out: bfloat16 [768, 1536], P('req'), may hold values from -0.21875 to 0.21875
- w_final: bfloat16 [1536, 64], replicated, may hold values from -0.15625 to 0.15625
- lengths: int32 [8], P('req'), may hold values from 16 to 154, as said below
- block_mask: int32 [8, 4, 4], P('req', 'blk'), may hold values from 0 to 1, as said below
- timestep: int32 [8], P('req'), may hold values from 0 to 27
- latent: float32 [8, 16, 32, 128], P('req', None, 'blk'), may hold values from -6 to 6
- conv_w: bfloat16 [512, 144], replicated, may hold values from -0.5 to 0.5
Outputs:
- velocity: float32 [8, 16, 32, 128], P('req', None, 'blk')
- latent_next: float32 [8, 16, 32, 128], P('req', None, 'blk')
- features: bfloat16 [8, 512, 32, 128], P('req', None, 'blk')
Inputs may be any that keep to these rules, and one draw needn't show every extreme that they name: Text keys from position lengths[r] on are padding; some request uses all 154 text tokens. Every tile may attend to its own keys: block_mask[r, t, t] = 1.
All inputs are finite; a program needn't handle non-finite values.
Results may differ from a plain program's by a relative error of at most 0.0063.
Values may be sent and summed in bfloat16 or wider, within the bound.
A program may use at most 192 MiB of HBM per device.

v0:
```python
import jax
import jax.numpy as jnp
from jax import lax
from jax.sharding import PartitionSpec as P

HD = 64
GRIDW = 64
PATCH = 2
LATC = 16
NSTEPS = 28
NORM_EPS = 1e-06
SHIFT_FACTOR = 3.0
LATENT_SCALE = 1.5305
LATENT_SHIFT = 0.0609
NEG_LARGE = -1e30
SCORE_SCALE = 0.125


def with_halo(block, sides, width):
    for axis, dim in sides:
        count = lax.axis_size(axis)
        forward = [(i, i + 1) for i in range(count - 1)]
        backward = [(target, source) for source, target in forward]
        low = lax.ppermute(
            lax.slice_in_dim(block, block.shape[dim] - width, None, axis=dim), axis, forward
        )
        high = lax.ppermute(lax.slice_in_dim(block, 0, width, axis=dim), axis, backward)
        block = jnp.concatenate([low, block, high], axis=dim)
    return block


def layer_norm(values):
    values = values.astype(jnp.float32)
    center = values - jnp.mean(values, axis=-1, keepdims=True)
    spread = jnp.mean(center * center, axis=-1, keepdims=True)
    return center * lax.rsqrt(spread + NORM_EPS)


def modulate(values, shift_row, scale_row):
    return layer_norm(values) * (1.0 + scale_row) + shift_row


def sigma_of(step_index, step_count):
    fraction = 1.0 - step_index.astype(jnp.float32) / step_count
    return SHIFT_FACTOR * fraction / (1.0 + (SHIFT_FACTOR - 1.0) * fraction)


def unpatchify(token_out, grid_width, patch_size, channels):
    patch_rows = token_out.shape[0] // grid_width
    shaped = token_out.reshape(patch_rows, grid_width, patch_size, patch_size, channels)
    shaped = jnp.transpose(shaped, (4, 0, 2, 1, 3))
    return shaped.reshape(channels, patch_rows * patch_size, grid_width * patch_size)


def convolve(padded, conv_w):
    row_count = padded.shape[1] - 2
    col_count = padded.shape[2] - 2
    tap_list = [
        padded[:, tap_row : tap_row + row_count, tap_col : tap_col + col_count]
        for tap_row in range(3)
        for tap_col in range(3)
    ]
    stacked = jnp.stack(tap_list, axis=1).reshape(padded.shape[0] * 9, row_count * col_count)
    convolved = jnp.dot(conv_w, stacked, preferred_element_type=jnp.float32)
    return convolved.reshape(conv_w.shape[0], row_count, col_count)


def text_state(queries, keys_txt, vals_txt, length):
    text_allowed = (jnp.arange(keys_txt.shape[0], dtype=jnp.int32) < length)[None, None, :]
    text_scores = (
        jnp.einsum("qhd,khd->qhk", queries, keys_txt, preferred_element_type=jnp.float32)
        * SCORE_SCALE
    )
    text_scores = jnp.where(text_allowed, text_scores, NEG_LARGE)
    text_max = jnp.max(text_scores, axis=2)
    text_weights = jnp.where(text_allowed, jnp.exp(text_scores - text_max[:, :, None]), 0.0)
    text_acc = jnp.einsum(
        "qhk,khd->qhd",
        text_weights.astype(jnp.bfloat16),
        vals_txt,
        preferred_element_type=jnp.float32,
    )
    return (text_max, jnp.sum(text_weights, axis=2), text_acc)


def absorb_block(previous, queries, head_keys, head_vals, allowed):
    old_max, old_sum, old_acc = previous
    scores = (
        jnp.einsum("qhd,khd->qhk", queries, head_keys, preferred_element_type=jnp.float32)
        * SCORE_SCALE
    )
    scores = jnp.where(allowed, scores, NEG_LARGE)
    new_max = jnp.maximum(old_max, jnp.max(scores, axis=2))
    weights = jnp.where(allowed, jnp.exp(scores - new_max[:, :, None]), 0.0)
    factor = jnp.exp(old_max - new_max)
    summed = jnp.einsum(
        "qhk,khd->qhd", weights.astype(jnp.bfloat16), head_vals, preferred_element_type=jnp.float32
    )
    return (
        new_max,
        old_sum * factor + jnp.sum(weights, axis=2),
        old_acc * factor[:, :, None] + summed,
    )


def absorb_maybe(previous, queries, head_keys, head_vals, allowed):
    return absorb_block(previous, queries, head_keys, head_vals, allowed)


def on_device(
    x_img,
    x_txt,
    modulation,
    w_img,
    w_txt,
    w_out,
    w_final,
    lengths,
    block_mask,
    timestep,
    latent,
    conv_w,
):
    tokens = x_img[0]
    factors = modulation[0]
    tok_rows = tokens.shape[0]
    head_cols = w_out.shape[0] * lax.axis_size("req")
    head_count = head_cols // HD
    h_img = modulate(tokens, factors[0], factors[1]).astype(jnp.bfloat16)
    h_txt = modulate(x_txt[0], factors[3], factors[4]).astype(jnp.bfloat16)
    qkv = jnp.dot(
        h_img, lax.all_gather(w_img, "req", axis=1, tiled=True), preferred_element_type=jnp.float32
    ).astype(jnp.bfloat16)
    kv_txt = jnp.dot(
        h_txt, lax.all_gather(w_txt, "req", axis=1, tiled=True), preferred_element_type=jnp.float32
    ).astype(jnp.bfloat16)
    keys_txt = kv_txt[:, :head_cols].reshape(-1, head_count, HD)
    vals_txt = kv_txt[:, head_cols:].reshape(-1, head_count, HD)
    length = lengths[0]
    queries = qkv[:, :head_cols].reshape(tok_rows, head_count, HD)
    keys_img = qkv[:, head_cols : 2 * head_cols]
    vals_img = qkv[:, 2 * head_cols :]
    mask_row = block_mask[0, 0]
    tile_count = mask_row.shape[0]
    start_state = text_state(queries, keys_txt, vals_txt, length)
    piece_keys = lax.all_gather(keys_img, "blk", axis=0, tiled=True)
    piece_vals = lax.all_gather(vals_img, "blk", axis=0, tiled=True)
    piece_len = piece_keys.shape[0]
    key_tile = jnp.arange(piece_len, dtype=jnp.int32) // tok_rows
    tile_hit = key_tile[:, None] == jnp.arange(tile_count, dtype=jnp.int32)[None, :]
    allowed = jnp.sum(jnp.where(tile_hit, mask_row[None, :], 0), axis=1) == 1
    head_keys = piece_keys.reshape(piece_len, head_count, HD)
    head_vals = piece_vals.reshape(piece_len, head_count, HD)
    run_max, run_sum, run_acc = absorb_maybe(
        start_state, queries, head_keys, head_vals, allowed[None, None, :]
    )
    attended = (run_acc / run_sum[:, :, None]).reshape(tok_rows, head_cols).astype(jnp.bfloat16)
    projected = jnp.dot(
        attended,
        lax.all_gather(w_out, "req", axis=0, tiled=True),
        preferred_element_type=jnp.float32,
    )
    residual = tokens.astype(jnp.float32) + factors[2] * projected
    final_in = modulate(residual, factors[5], factors[6]).astype(jnp.bfloat16)
    token_out = jnp.dot(final_in, w_final, preferred_element_type=jnp.float32)
    velocity = unpatchify(token_out, GRIDW, PATCH, LATC)[None]
    step_index = timestep[0]
    sigma_step = sigma_of(step_index + 1, NSTEPS) - sigma_of(step_index, NSTEPS)
    latent_next = latent + sigma_step * velocity
    decoded = (latent_next / LATENT_SCALE + LATENT_SHIFT).astype(jnp.bfloat16)
    padded = with_halo(decoded, (("blk", 2),), 1)
    padded = jnp.pad(padded[0], ((0, 0), (0, 0), (1, 1)))
    features = convolve(padded, conv_w).astype(jnp.bfloat16)[None]
    return (velocity, latent_next, features)


def solution(mesh):
    return jax.shard_map(
        on_device,
        mesh=mesh,
        in_specs=(
            P("req", "blk", None),
            P("req", None, None),
            P("req", None, None),
            P(None, "req"),
            P(None, "req"),
            P("req", None),
            P(),
            P("req"),
            P("req", "blk", None),
            P("req"),
            P("req", None, "blk", None),
            P(),
        ),
        out_specs=(
            P("req", None, "blk", None),
            P("req", None, "blk", None),
            P("req", None, "blk", None),
        ),
        check_vma=False,
    )
```

profile of v0, /device:TPU:0, one launch (start us, length us, event | category | flops | bytes accessed | tf_op | source)
XLA Modules:
  0.0 230.1 jit_solution(16971153236048344387)
XLA Ops:
  7.2 0.7 all-gather.8.cloned.1.call-update
  8.0 0.7 all-gather.6.cloned.1.call-update
  8.7 0.9 add_reduce_fusion
  9.6 0.2 convert_reduce_fusion
  9.8 0.3 fusion.14
  10.2 51.3 %all-gather.8.cloned.1.call-done = bf16[1536,2304]{0,1:T(8,128)(2,1)} async-done(((bf16[1536,288]{0,1:T(8,128)(2,1)}), bf16[1536,2304]{0,1:T(8,128)(2,1)}) %all-gather.8.cloned.1.call-update) | async-done | bytes 7077904 | tf_op jit(solution)/shard_map/all_gather | solution.py:132
  61.5 5.2 %convolution_convert_fusion = bf16[256,2304]{1,0:T(8,128)(2,1)S(1)} fusion(bf16[1536,2304]{0,1:T(8,128)(2,1)} %all-gather.8.cloned.1.call-done, bf16[1,256,1536]{2,1,0:T(8,128)(2,1)S(1)} %copy-done.2, f32[1536]{0:T(1024)S(1)} %get-tuple-element.16, f32[1536]{0:T(1024)S(1)} %get-tuple-element.17, f32[256]{0:T(256)S(1)} %add_rsqrt_fusion.1, ...), kind=kOutput, calls=%fused_computation.10 | convolution fusion | flops 1814888448 | bytes 9058304 | tf_op jit(solution)/shard_map/dot_general | solution.py:131
  66.7 1.0 fusion.69
  67.7 0.5 all-gather.12.cloned.1.call-update
  68.3 0.5 all-gather.14.cloned.1.call-update
  69.5 0.1 convert_reduce_fusion.1
  69.7 0.3 fusion.30
  70.7 0.1 select_reduce_fusion
  70.8 1.0 copy.66
  71.9 30.4 %all-gather.6.cloned.1.call-done = bf16[1536,1536]{0,1:T(8,128)(2,1)} async-done(((bf16[1536,192]{0,1:T(8,128)(2,1)}), bf16[1536,1536]{0,1:T(8,128)(2,1)}) %all-gather.6.cloned.1.call-update) | async-done | bytes 4718608 | tf_op jit(solution)/shard_map/all_gather | solution.py:135
  102.3 4.0 %convolution_convert_fusion.1 = bf16[154,1536]{1,0:T(8,128)(2,1)S(1)} fusion(bf16[1536,1536]{0,1:T(8,128)(2,1)} %all-gather.6.cloned.1.call-done, bf16[1,154,1536]{2,1,0:T(8,128)(2,1)S(1)} %copy-done.4, f32[1536]{0:T(1024)S(1)} %get-tuple-element.18, f32[1536]{0:T(1024)S(1)} %get-tuple-element.19, f32[154]{0:T(256)S(1)} %add_rsqrt_fusion.2, ...), kind=kOutput, calls=%fused_computation.13 | convolution fusion | flops 728318976 | bytes 5678288 | tf_op jit(solution)/shard_map/dot_general | solution.py:134
  106.4 0.9 copy.60
  107.3 0.9 copy.59
  108.3 0.2 copy.61
  108.4 1.6 bitcast_reduce_fusion.1
  110.0 0.6 fusion.18
  110.6 30.5 %all-gather.10.cloned.1.call-done = bf16[1024,768]{1,0:T(8,128)(2,1)} async-done(((bf16[256,768]{1,0:T(8,128)(2,1)}), bf16[1024,768]{1,0:T(8,128)(2,1)}) %all-gather.10.cloned.1.call-update) | async-done | bytes 1572880 | tf_op jit(solution)/shard_map/all_gather | solution.py:146
  141.0 2.6 %copy.62 = bf16[1024,768]{0,1:T(8,128)(2,1)} copy(bf16[1024,768]{1,0:T(8,128)(2,1)} %all-gather.10.cloned.1.call-done) | data formatting | bytes 3145728 | tf_op jit(solution)/shard_map/all_gather | solution.py:146
  143.6 8.8 %bitcast_reduce_fusion = (f32[256,12]{0,1:T(8,128)S(1)}, f32[12,1024,256]{2,1,0:T(8,128)}) fusion(pred[1024]{0:T(1024)(128)(4,1)S(1)} %broadcast_compare_fusion, bf16[1024,12,64]{0,2,1:T(8,128)(2,1)} %bitcast.129, bf16[256,12,64]{0,2,1:T(8,128)(2,1)S(1)} %bitcast.134), kind=kOutput, calls=%fused_computation.1 | convolution fusion | flops 412087296 | bytes 14562304 | tf_op jit(solution)/shard_map/qhd,khd->qhk/dot_general | solution.py:89
  152.5 26.0 %all-gather.12.cloned.1.call-done = bf16[1024,768]{1,0:T(8,128)(2,1)} async-done(((bf16[256,768]{1,0:T(8,128)(2,1)}), bf16[1024,768]{1,0:T(8,128)(2,1)}) %all-gather.12.cloned.1.call-update) | async-done | bytes 1572880 | tf_op jit(solution)/shard_map/all_gather | solution.py:147
  178.4 2.6 %copy.63 = bf16[1024,768]{0,1:T(8,128)(2,1)} copy(bf16[1024,768]{1,0:T(8,128)(2,1)} %all-gather.12.cloned.1.call-done) | data formatting | bytes 3145728 | tf_op jit(solution)/shard_map/all_gather | solution.py:147
  181.0 7.2 %fusion.2 = f32[256,12]{0,1:T(8,128)S(1)} fusion(f32[12,1024,256]{2,1,0:T(8,128)} %get-tuple-element.45, f32[256,12]{0,1:T(8,128)S(1)} %max.13, pred[1024]{0:T(1024)(128)(4,1)S(1)} %broadcast_compare_fusion), kind=kLoop, calls=%fused_computation.5 | loop fusion | flops 15725568 | bytes 12608512 | tf_op jit(solution)/shard_map/reduce_sum | solution.py:101
  188.3 1.3 copy-done.1
  189.6 4.3 %fusion.20 = f32[256,12,64]{0,2,1:T(8,128)S(1)} fusion(bf16[1024,12,64]{0,2,1:T(8,128)(2,1)} %bitcast.135, f32[12,1024,256]{2,1,0:T(8,128)S(1)} %copy-done.1, f32[256,12]{0,1:T(8,128)S(1)} %max.13, pred[1024]{0:T(1024)(128)(4,1)S(1)} %broadcast_compare_fusion), kind=kOutput, calls=%fused_computation.33 | convolution fusion | flops 418381824 | bytes 14955520 | tf_op jit(solution)/shard_map/qhk,khd->qhd/dot_general | solution.py:96
  193.9 0.7 fusion.26
  194.6 13.5 %all-gather.14.cloned.1.call-done = bf16[768,1536]{1,0:T(8,128)(2,1)} async-done(((bf16[96,1536]{1,0:T(8,128)(2,1)}), bf16[768,1536]{1,0:T(8,128)(2,1)}) %all-gather.14.cloned.1.call-update) | async-done | bytes 2359312 | tf_op jit(solution)/shard_map/all_gather | solution.py:160
  208.1 2.5 %fusion.72 = (f32[256]{0:T(256)S(1)}, f32[256,1536]{1,0:T(8,128)S(1)}) fusion(bf16[256,768]{0,1:T(8,128)(2,1)S(1)} %bitcast.137, bf16[768,1536]{1,0:T(8,128)(2,1)} %all-gather.14.cloned.1.call-done, f32[1536]{0:T(1024)S(1)} %get-tuple-element.20, bf16[1,256,1536]{2,1,0:T(8,128)(2,1)S(1)} %copy-done.2), kind=kOutput, calls=%fused_computation.127 | convolution fusion | flops 605552384 | bytes 5118976 | tf_op jit(solution)/shard_map/dot_general | solution.py:158
  210.6 0.3 multiply_reduce_fusion
  211.0 0.5 fusion.46
  211.4 0.1 reshape.190
  211.6 0.3 copy.65
  211.9 0.1 add_convert_fusion.2
  212.0 3.4 %collective-permute-start = (bf16[1,16,1,128]{1,3,2,0:T(8,128)(2,1)S(1)}, bf16[1,16,1,128]{1,3,2,0:T(8,128)(2,1)S(1)}, u32[]{:S(2)}, u32[]{:S(2)}) collective-permute-start(bf16[1,16,1,128]{1,3,2,0:T(8,128)(2,1)S(1)} %get-tuple-element.31), channel_id=1, source_target_pairs={{0,1},{1,2},{2,3},{4,5},{5,6},{6,7},{8,9},{9,10},{10,11},{12,13},{... | collective-permute-start | bytes 12296 | tf_op jit(solution)/shard_map/ppermute | solution.py:24
  215.4 1.3 collective-permute-start.1
  216.7 0.1 copy.68
  216.8 0.8 copy.79
  217.6 0.8 copy.80
  218.4 0.1 copy.67
  218.5 2.7 %collective-permute-done.1 = bf16[1,16,1,128]{1,3,2,0:T(8,128)(2,1)S(1)} collective-permute-done((bf16[1,16,1,128]{1,3,2,0:T(8,128)(2,1)S(1)}, bf16[1,16,1,128]{1,3,2,0:T(8,128)(2,1)S(1)}, u32[]{:S(2)}, u32[]{:S(2)}) %collective-permute-start.1) | collective-permute-done | bytes 4128 | tf_op jit(solution)/shard_map/ppermute | solution.py:27
  221.2 0.1 copy.69
  221.3 0.1 fusion.59
  221.6 0.5 convolution_convert_fusion.2
  222.1 1.5 copy.81
  (47 shorter events, 0.6 us)
Async XLA Ops:
  7.2 203.8 %copy-start = (bf16[1536,64]{0,1:T(8,128)(2,1)S(1)}, bf16[1536,64]{0,1:T(8,128)(2,1)}, u32[]{:S(2)}) copy-start(bf16[1536,64]{0,1:T(8,128)(2,1)} %param.18) | copy-start | bytes 589828
  7.2 2.5 %copy-start.2 = (bf16[1,256,1536]{2,1,0:T(8,128)(2,1)S(1)}, bf16[1,256,1536]{2,1,0:T(8,128)(2,1)}, u32[]{:S(2)}) copy-start(bf16[1,256,1536]{2,1,0:T(8,128)(2,1)} %param.12) | copy-start | bytes 2359300
  7.2 54.3 %all-gather.8.cloned.1.call-start = ((), (), s32[]{:S(2)}) async-start(), calls=%async_computation.1 | async-start | bytes 7962624 | tf_op jit(solution)/shard_map/all_gather | solution.py:132
  7.9 94.4 %all-gather.6.cloned.1.call-start = ((), (), s32[]{:S(2)}) async-start(), calls=%async_computation | async-start | bytes 5308416 | tf_op jit(solution)/shard_map/all_gather | solution.py:135
  8.7 132.4 %all-gather.10.cloned.1.call-start = ((), (), s32[]{:S(2)}) async-start(), calls=%async_computation.2 | async-start | bytes 1966080 | tf_op jit(solution)/shard_map/all_gather | solution.py:146
  66.7 2.9 %copy-start.4 = (bf16[1,154,1536]{2,1,0:T(8,128)(2,1)S(1)}, bf16[1,154,1536]{2,1,0:T(8,128)(2,1)}, u32[]{:S(2)}) copy-start(bf16[1,154,1536]{2,1,0:T(8,128)(2,1)} %param.13) | copy-start | bytes 1419268
  66.7 4.0 %copy-start.8 = (s32[1,1,4]{2,1,0:T(1,128)S(1)}, s32[1,1,4]{2,1,0:T(1,128)}, u32[]{:S(2)}) copy-start(s32[1,1,4]{2,1,0:T(1,128)} %param.20) | copy-start | bytes 52
  66.7 4.1 %copy-start.7 = (f32[1,16,8,128]{3,2,1,0:T(8,128)S(1)}, f32[1,16,8,128]{3,2,1,0:T(8,128)}, u32[]{:S(2)}) copy-start(f32[1,16,8,128]{3,2,1,0:T(8,128)} %param.22) | copy-start | bytes 196612
  67.7 110.8 %all-gather.12.cloned.1.call-start = ((), (), s32[]{:S(2)}) async-start(), calls=%async_computation.3 | async-start | bytes 1966080 | tf_op jit(solution)/shard_map/all_gather | solution.py:147
  68.3 139.8 %all-gather.14.cloned.1.call-start = ((), (), s32[]{:S(2)}) async-start(), calls=%async_computation.4 | async-start | bytes 2654208 | tf_op jit(solution)/shard_map/all_gather | solution.py:160
  181.0 8.5 %copy-start.1 = (f32[12,1024,256]{2,1,0:T(8,128)S(1)}, f32[12,1024,256]{2,1,0:T(8,128)}, u32[]{:S(2)}) copy-start(f32[12,1024,256]{2,1,0:T(8,128)} %get-tuple-element.45) | copy-start | bytes 37748740
  189.6 4.3 %copy-start.5 = (bf16[154,768]{0,1:T(8,128)(2,1)S(1)}, bf16[154,768]{0,1:T(8,128)(2,1)}, u32[]{:S(2)}) copy-start(bf16[154,768]{0,1:T(8,128)(2,1)} %copy.59) | copy-start | bytes 709636
  210.6 1.2 copy-start.3
  211.8 9.8 %copy-start.6 = (bf16[512,144]{0,1:T(8,128)(2,1)S(1)}, bf16[512,144]{0,1:T(8,128)(2,1)}, u32[]{:S(2)}) copy-start(bf16[512,144]{0,1:T(8,128)(2,1)} %param.23) | copy-start | bytes 442372
  212.0 6.4 %collective-permute-start = (bf16[1,16,1,128]{1,3,2,0:T(8,128)(2,1)S(1)}, bf16[1,16,1,128]{1,3,2,0:T(8,128)(2,1)S(1)}, u32[]{:S(2)}, u32[]{:S(2)}) collective-permute-start(bf16[1,16,1,128]{1,3,2,0:T(8,128)(2,1)S(1)} %get-tuple-element.31), channel_id=1, source_target_pairs={{0,1},{1,2},{2,3},{4,5},{5,6},{6,7},{8,9},{9,10},{10,11},{12,13},{... | collective-permute-start | bytes 12296 | tf_op jit(solution)/shard_map/ppermute | solution.py:24
  215.4 5.8 %collective-permute-start.1 = (bf16[1,16,1,128]{1,3,2,0:T(8,128)(2,1)S(1)}, bf16[1,16,1,128]{1,3,2,0:T(8,128)(2,1)S(1)}, u32[]{:S(2)}, u32[]{:S(2)}) collective-permute-start(bf16[1,16,1,128]{1,3,2,0:T(8,128)(2,1)S(1)} %get-tuple-element.32), channel_id=1, source_target_pairs={{1,0},{2,1},{3,2},{5,4},{6,5},{7,6},{9,8},{10,9},{11,10},{13,12},{... | collective-permute-start | bytes 12296 | tf_op jit(solution)/shard_map/ppermute | solution.py:27
Sparse Core Ops, SparseCore 0:
  9.9 51.5 all-gather.7
  63.4 38.9 all-gather.5
  103.9 37.0 all-gather.9
  142.5 35.9 all-gather.11
  180.2 27.8 all-gather.13
where the time goes:
time: 231 us; the launch traced here: 230 us
  waiting for transfers between devices  157 us (68%)
  matrix products  28 us (12%)
  between operations  15.5 us (7%)
  local copies, waits for them, and re-layouts  14.5 us (6%)
  other arithmetic  10.2 us (4%)
  starting transfers between devices  4.88 us (2%)
    all_gather x1, waiting for transfers between devices, on_device(): lax.all_gather(w_img, 'req', axis=1, tiled=True)  51.3 us
    all_gather x1, waiting for transfers between devices, on_device(): piece_keys = lax.all_gather(keys_img, 'blk', axis=0, tiled=True)  30.5 us
    all_gather x1, waiting for transfers between devices, on_device(): lax.all_gather(w_txt, 'req', axis=1, tiled=True)  30.4 us
    all_gather x1, waiting for transfers between devices, on_device(): piece_vals = lax.all_gather(vals_img, 'blk', axis=0, tiled=True)  26 us
    all_gather x1, waiting for transfers between devices, on_device(): lax.all_gather(w_out, 'req', axis=0, tiled=True)  13.5 us
    dot_general x1, matrix products, absorb_block(): jnp.einsum('qhd,khd->qhk', queries, head_keys, preferred_element_type=jnp...  8.82 us
    reduce_sum x1, other arithmetic, absorb_block(): jnp.sum(weights, axis=2)  7.21 us
    unnamed x30, local copies, waits for them, and re-layouts  5.57 us
  transfers between devices with their start and end apart: 7, of which 6 were waited for; matrix products, arithmetic and copies ran while one was open for 20% of the time, Pallas kernels for 0%

commit v1 on v0

--- a/solution.py
+++ b/solution.py
@@ -143,8 +143,11 @@
     mask_row = block_mask[0, 0]
     tile_count = mask_row.shape[0]
     start_state = text_state(queries, keys_txt, vals_txt, length)
-    piece_keys = lax.all_gather(keys_img, "blk", axis=0, tiled=True)
-    piece_vals = lax.all_gather(vals_img, "blk", axis=0, tiled=True)
+    piece_keys, piece_vals = jnp.split(
+        lax.all_gather(jnp.concatenate([keys_img, vals_img], axis=1), "blk", axis=0, tiled=True),
+        [keys_img.shape[1]],
+        axis=1,
+    )
     piece_len = piece_keys.shape[0]
     key_tile = jnp.arange(piece_len, dtype=jnp.int32) // tok_rows
     tile_hit = key_tile[:, None] == jnp.arange(tile_count, dtype=jnp.int32)[None, :]

time: 231 us -> 220 us (0.952)
  waiting for transfers between devices: 157 us -> 145 us
  local copies, waits for them, and re-layouts: 14.5 us -> 18.3 us
    all_gather x1, waiting for transfers between devices: 13.5 us -> 0.02 us  [on_device(): lax.all_gather(w_out, 'req', axis=0, tiled=True)]
    split x0 -> x3, local copies, waits for them, and re-layouts: none -> 8.96 us  [on_device(): jnp.split(lax.all_gather(jnp.concatenate([keys_img, vals_img], axis=1), '...]
    all_gather x2 -> x0, local copies, waits for them, and re-layouts: 5.2 us -> none  [the longest x1 2.6 us: on_device(): piece_keys = lax.all_gather(keys_img, 'blk', axis=0, tiled=True)]
    all_gather x2 -> x1, waiting for transfers between devices: 56.5 us -> 57.4 us  [on_device(): lax.all_gather(jnp.concatenate([keys_img, vals_img], axis=1), 'blk', axis...]
  transfers between devices with their start and end apart: 7 -> 6, of which waited for: 6 -> 4; matrix products, arithmetic and copies ran while one was open for 20% -> 22% of each run, Pallas kernels for 0% -> 0%
where the time goes in v1:
time: 220 us
  waiting for transfers between devices  145 us (66%)
  matrix products  28.1 us (13%)
  local copies, waits for them, and re-layouts  18.3 us (8%)
  between operations  15.5 us (7%)
  other arithmetic  10.4 us (5%)
  starting transfers between devices  2.74 us (1%)
    all_gather x1, waiting for transfers between devices, on_device(): lax.all_gather(jnp.concatenate([keys_img, vals_img], axis=1), 'blk', axis...  57.4 us
    all_gather x1, waiting for transfers between devices, on_device(): lax.all_gather(w_img, 'req', axis=1, tiled=True)  51.3 us
    all_gather x1, waiting for transfers between devices, on_device(): lax.all_gather(w_txt, 'req', axis=1, tiled=True)  31.1 us
    split x3, local copies, waits for them, and re-layouts, on_device(): jnp.split(lax.all_gather(jnp.concatenate([keys_img, vals_img], axis=1), '...  8.96 us
    dot_general x1, matrix products, absorb_block(): jnp.einsum('qhd,khd->qhk', queries, head_keys, preferred_element_type=jnp...  8.88 us
    reduce_sum x1, other arithmetic, absorb_block(): jnp.sum(weights, axis=2)  7.42 us
    unnamed x30, local copies, waits for them, and re-layouts  5.58 us
    dot_general x1, matrix products, on_device(): jnp.dot(h_img, lax.all_gather(w_img, 'req', axis=1, tiled=True), preferre...  5.16 us
  transfers between devices with their start and end apart: 6, of which 4 were waited for; matrix products, arithmetic and copies ran while one was open for 22% of the time, Pallas kernels for 0%

profile of v1, /device:TPU:0, one launch (start us, length us, event | category | flops | bytes accessed | tf_op | source)
XLA Modules:
  0.0 219.7 jit_solution(10724856641224826074)
XLA Ops:
  7.2 0.7 all-gather.7.cloned.1.call-update
  8.0 0.7 all-gather.5.cloned.1.call-update
  8.7 0.0 all-gather.9.cloned.1.call-start
  8.7 0.9 add_reduce_fusion
  9.6 0.2 convert_reduce_fusion
  9.8 0.3 fusion.14
  10.2 51.3 %all-gather.7.cloned.1.call-done = bf16[1536,2304]{0,1:T(8,128)(2,1)} async-done(((bf16[1536,288]{0,1:T(8,128)(2,1)}), bf16[1536,2304]{0,1:T(8,128)(2,1)}) %all-gather.7.cloned.1.call-update) | async-done | bytes 7077904 | tf_op jit(solution)/shard_map/all_gather | solution.py:132
  61.5 5.2 %convolution_convert_fusion = bf16[256,2304]{1,0:T(8,128)(2,1)S(1)} fusion(bf16[1536,2304]{0,1:T(8,128)(2,1)} %all-gather.7.cloned.1.call-done, bf16[1,256,1536]{2,1,0:T(8,128)(2,1)S(1)} %copy-done.2, f32[1536]{0:T(1024)S(1)} %get-tuple-element.16, f32[1536]{0:T(1024)S(1)} %get-tuple-element.17, f32[256]{0:T(256)S(1)} %add_rsqrt_fusion.1, ...), kind=kOutput, calls=%fused_computation.10 | convolution fusion | flops 1814888448 | bytes 9058304 | tf_op jit(solution)/shard_map/dot_general | solution.py:131
  66.7 0.9 concatenate.8
  67.7 0.0 all-gather.11.cloned.1.call-start
  67.7 0.5 all-gather.11.cloned.1.call-update
  68.9 0.1 convert_reduce_fusion.1
  69.1 0.3 fusion.30
  70.0 0.1 select_reduce_fusion
  70.2 1.0 copy.66
  71.3 31.1 %all-gather.5.cloned.1.call-done = bf16[1536,1536]{0,1:T(8,128)(2,1)} async-done(((bf16[1536,192]{0,1:T(8,128)(2,1)}), bf16[1536,1536]{0,1:T(8,128)(2,1)}) %all-gather.5.cloned.1.call-update) | async-done | bytes 4718608 | tf_op jit(solution)/shard_map/all_gather | solution.py:135
  102.4 4.0 %convolution_convert_fusion.1 = bf16[154,1536]{1,0:T(8,128)(2,1)S(1)} fusion(bf16[1536,1536]{0,1:T(8,128)(2,1)} %all-gather.5.cloned.1.call-done, bf16[1,154,1536]{2,1,0:T(8,128)(2,1)S(1)} %copy-done.4, f32[1536]{0:T(1024)S(1)} %get-tuple-element.18, f32[1536]{0:T(1024)S(1)} %get-tuple-element.19, f32[154]{0:T(256)S(1)} %add_rsqrt_fusion.2, ...), kind=kOutput, calls=%fused_computation.13 | convolution fusion | flops 728318976 | bytes 5678288 | tf_op jit(solution)/shard_map/dot_general | solution.py:134
  106.4 0.9 copy.60
  107.4 0.9 copy.59
  108.3 0.2 copy.61
  108.5 1.6 bitcast_reduce_fusion.1
  110.0 0.6 fusion.18
  110.6 57.4 %all-gather.9.cloned.1.call-done = bf16[1024,1536]{1,0:T(8,128)(2,1)} async-done(((bf16[256,1536]{1,0:T(8,128)(2,1)}), bf16[1024,1536]{1,0:T(8,128)(2,1)}) %all-gather.9.cloned.1.call-update) | async-done | bytes 3145744 | tf_op jit(solution)/shard_map/all_gather | solution.py:147
  168.0 3.8 %fusion.69 = (bf16[1024,768]{1,0:T(8,128)(2,1)}, bf16[1024,768]{1,0:T(8,128)(2,1)}) fusion(bf16[1024,1536]{1,0:T(8,128)(2,1)} %all-gather.9.cloned.1.call-done), kind=kLoop, calls=%fused_computation.124 | loop fusion | bytes 6291456 | tf_op jit(solution)/shard_map/split | solution.py:146
  171.8 2.6 %copy.62 = bf16[1024,768]{0,1:T(8,128)(2,1)} copy(bf16[1024,768]{1,0:T(8,128)(2,1)} %get-tuple-element.26) | data formatting | bytes 3145728 | tf_op jit(solution)/shard_map/split | solution.py:146
  174.4 8.9 %bitcast_reduce_fusion = (f32[256,12]{0,1:T(8,128)S(1)}, f32[12,1024,256]{2,1,0:T(8,128)}) fusion(pred[1024]{0:T(1024)(128)(4,1)S(1)} %broadcast_compare_fusion, bf16[1024,12,64]{0,2,1:T(8,128)(2,1)} %bitcast.129, bf16[256,12,64]{0,2,1:T(8,128)(2,1)S(1)} %bitcast.134), kind=kOutput, calls=%fused_computation.1 | convolution fusion | flops 412087296 | bytes 14562304 | tf_op jit(solution)/shard_map/qhd,khd->qhk/dot_general | solution.py:89
  183.3 2.6 %copy.63 = bf16[1024,768]{0,1:T(8,128)(2,1)} copy(bf16[1024,768]{1,0:T(8,128)(2,1)} %get-tuple-element.27) | data formatting | bytes 3145728 | tf_op jit(solution)/shard_map/split | solution.py:146
  185.9 7.4 %fusion.2 = f32[256,12]{0,1:T(8,128)S(1)} fusion(f32[12,1024,256]{2,1,0:T(8,128)} %get-tuple-element.44, f32[256,12]{0,1:T(8,128)S(1)} %max.13, pred[1024]{0:T(1024)(128)(4,1)S(1)} %broadcast_compare_fusion), kind=kLoop, calls=%fused_computation.5 | loop fusion | flops 15725568 | bytes 12608512 | tf_op jit(solution)/shard_map/reduce_sum | solution.py:101
  193.3 1.3 copy-done.1
  194.6 4.3 %fusion.20 = f32[256,12,64]{0,2,1:T(8,128)S(1)} fusion(bf16[1024,12,64]{0,2,1:T(8,128)(2,1)} %bitcast.135, f32[12,1024,256]{2,1,0:T(8,128)S(1)} %copy-done.1, f32[256,12]{0,1:T(8,128)S(1)} %max.13, pred[1024]{0:T(1024)(128)(4,1)S(1)} %broadcast_compare_fusion), kind=kOutput, calls=%fused_computation.33 | convolution fusion | flops 418381824 | bytes 14955520 | tf_op jit(solution)/shard_map/qhk,khd->qhd/dot_general | solution.py:96
  199.0 0.7 fusion.26
  199.6 2.5 %fusion.72 = (f32[256]{0:T(256)S(1)}, f32[256,1536]{1,0:T(8,128)S(1)}) fusion(bf16[256,768]{0,1:T(8,128)(2,1)S(1)} %bitcast.137, bf16[768,1536]{1,0:T(8,128)(2,1)} %all-gather.11.cloned.1.call-done, f32[1536]{0:T(1024)S(1)} %get-tuple-element.20, bf16[1,256,1536]{2,1,0:T(8,128)(2,1)S(1)} %copy-done.2), kind=kOutput, calls=%fused_computation.127 | convolution fusion | flops 605552384 | bytes 5118976 | tf_op jit(solution)/shard_map/dot_general | solution.py:161
  202.2 0.3 multiply_reduce_fusion
  202.5 0.5 fusion.46
  203.0 0.1 reshape.190
  203.1 0.3 copy.65
  203.4 0.1 add_convert_fusion.2
  203.5 1.3 collective-permute-start
  204.8 1.3 collective-permute-start.1
  206.1 0.1 copy.68
  206.3 0.8 copy.79
  207.1 0.8 copy.80
  207.9 0.1 copy.67
  207.9 2.8 %collective-permute-done.1 = bf16[1,16,1,128]{1,3,2,0:T(8,128)(2,1)S(1)} collective-permute-done((bf16[1,16,1,128]{1,3,2,0:T(8,128)(2,1)S(1)}, bf16[1,16,1,128]{1,3,2,0:T(8,128)(2,1)S(1)}, u32[]{:S(2)}, u32[]{:S(2)}) %collective-permute-start.1) | collective-permute-done | bytes 4128 | tf_op jit(solution)/shard_map/ppermute | solution.py:27
  210.8 0.1 copy.69
  210.9 0.1 fusion.59
  211.2 0.5 convolution_convert_fusion.2
  211.7 1.5 copy.81
  (46 shorter events, 0.5 us)
Async XLA Ops:
  7.2 195.4 %copy-start = (bf16[1536,64]{0,1:T(8,128)(2,1)S(1)}, bf16[1536,64]{0,1:T(8,128)(2,1)}, u32[]{:S(2)}) copy-start(bf16[1536,64]{0,1:T(8,128)(2,1)} %param.18) | copy-start | bytes 589828
  7.2 2.5 %copy-start.2 = (bf16[1,256,1536]{2,1,0:T(8,128)(2,1)S(1)}, bf16[1,256,1536]{2,1,0:T(8,128)(2,1)}, u32[]{:S(2)}) copy-start(bf16[1,256,1536]{2,1,0:T(8,128)(2,1)} %param.12) | copy-start | bytes 2359300
  7.2 54.3 %all-gather.7.cloned.1.call-start = ((), (), s32[]{:S(2)}) async-start(), calls=%async_computation.1 | async-start | bytes 7962624 | tf_op jit(solution)/shard_map/all_gather | solution.py:132
  7.9 94.4 %all-gather.5.cloned.1.call-start = ((), (), s32[]{:S(2)}) async-start(), calls=%async_computation | async-start | bytes 5308416 | tf_op jit(solution)/shard_map/all_gather | solution.py:135
  8.7 159.4 %all-gather.9.cloned.1.call-start = ((), (), s32[]{:S(2)}) async-start(), calls=%async_computation.2 | async-start | bytes 3932160 | tf_op jit(solution)/shard_map/all_gather | solution.py:147
  66.7 2.2 %copy-start.4 = (bf16[1,154,1536]{2,1,0:T(8,128)(2,1)S(1)}, bf16[1,154,1536]{2,1,0:T(8,128)(2,1)}, u32[]{:S(2)}) copy-start(bf16[1,154,1536]{2,1,0:T(8,128)(2,1)} %param.13) | copy-start | bytes 1419268
  66.7 3.4 %copy-start.8 = (s32[1,1,4]{2,1,0:T(1,128)S(1)}, s32[1,1,4]{2,1,0:T(1,128)}, u32[]{:S(2)}) copy-start(s32[1,1,4]{2,1,0:T(1,128)} %param.20) | copy-start | bytes 52
  66.7 3.5 %copy-start.7 = (f32[1,16,8,128]{3,2,1,0:T(8,128)S(1)}, f32[1,16,8,128]{3,2,1,0:T(8,128)}, u32[]{:S(2)}) copy-start(f32[1,16,8,128]{3,2,1,0:T(8,128)} %param.22) | copy-start | bytes 196612
  67.7 132.0 %all-gather.11.cloned.1.call-start = ((), (), s32[]{:S(2)}) async-start(), calls=%async_computation.3 | async-start | bytes 2654208 | tf_op jit(solution)/shard_map/all_gather | solution.py:163
  185.9 8.7 %copy-start.1 = (f32[12,1024,256]{2,1,0:T(8,128)S(1)}, f32[12,1024,256]{2,1,0:T(8,128)}, u32[]{:S(2)}) copy-start(f32[12,1024,256]{2,1,0:T(8,128)} %get-tuple-element.44) | copy-start | bytes 37748740
  194.6 4.3 %copy-start.5 = (bf16[154,768]{0,1:T(8,128)(2,1)S(1)}, bf16[154,768]{0,1:T(8,128)(2,1)}, u32[]{:S(2)}) copy-start(bf16[154,768]{0,1:T(8,128)(2,1)} %copy.59) | copy-start | bytes 709636
  202.2 1.2 copy-start.3
  203.4 7.8 %copy-start.6 = (bf16[512,144]{0,1:T(8,128)(2,1)S(1)}, bf16[512,144]{0,1:T(8,128)(2,1)}, u32[]{:S(2)}) copy-start(bf16[512,144]{0,1:T(8,128)(2,1)} %param.23) | copy-start | bytes 442372
  203.5 4.3 %collective-permute-start = (bf16[1,16,1,128]{1,3,2,0:T(8,128)(2,1)S(1)}, bf16[1,16,1,128]{1,3,2,0:T(8,128)(2,1)S(1)}, u32[]{:S(2)}, u32[]{:S(2)}) collective-permute-start(bf16[1,16,1,128]{1,3,2,0:T(8,128)(2,1)S(1)} %get-tuple-element.30), channel_id=1, source_target_pairs={{0,1},{1,2},{2,3},{4,5},{5,6},{6,7},{8,9},{9,10},{10,11},{12,13},{... | collective-permute-start | bytes 12296 | tf_op jit(solution)/shard_map/ppermute | solution.py:24
  204.8 5.9 %collective-permute-start.1 = (bf16[1,16,1,128]{1,3,2,0:T(8,128)(2,1)S(1)}, bf16[1,16,1,128]{1,3,2,0:T(8,128)(2,1)S(1)}, u32[]{:S(2)}, u32[]{:S(2)}) collective-permute-start(bf16[1,16,1,128]{1,3,2,0:T(8,128)(2,1)S(1)} %get-tuple-element.31), channel_id=1, source_target_pairs={{1,0},{2,1},{3,2},{5,4},{6,5},{7,6},{9,8},{10,9},{11,10},{13,12},{... | collective-permute-start | bytes 12296 | tf_op jit(solution)/shard_map/ppermute | solution.py:27
Sparse Core Ops, SparseCore 0:
  9.9 51.5 all-gather.6
  63.4 38.9 all-gather.4
  104.5 63.4 all-gather.8
  169.8 27.6 all-gather.10
